TPU v7x, 32 devices: a whole 2x2x4 slice. The times are simulated.
32 devices in a mesh: seq: 8 (over z, core), fsdp: 4 (over y, x).
Axes of the slice: x: 2, y: 2, z: 4, core: 2. Of those that a mesh axis runs over, the one named last changes fastest.
Arguments:
- hidden: bfloat16 [4, 1280, 2048], P('fsdp', 'seq'), may hold values from -6 to 6
- lengths: int32 [4, 4], replicated, may hold values from 1 to 1024, 1280 in all within a row
- w_input: bfloat16 [2048, 2048], P(None, 'fsdp'), may hold values from -0.125 to 0.125
- w_forget: bfloat16 [2048, 2048], P(None, 'fsdp'), may hold values from -0.125 to 0.125
- w_gate_out: bfloat16 [2048, 2048], P(None, 'fsdp'), may hold values from -0.125 to 0.125
- w_output: bfloat16 [2048, 2048], P('fsdp'), may hold values from -0.25 to 0.25
- norm_gain: float32 [2048], replicated, may hold values from 0.5 to 1.5
- gate_gain: float32 [2048], replicated, may hold values from 0.5 to 1.5
- glu_gain: float32 [2048], replicated, may hold values from 0.5 to 1.5
- lower_table: float32 [24, 2048], replicated, may hold values from -12 to 12
- w_glu_gate: bfloat16 [2048, 5632], P(None, 'fsdp'), may hold values from -0.125 to 0.125
- w_glu_up: bfloat16 [2048, 5632], P(None, 'fsdp'), may hold values from -0.125 to 0.125
- w_glu_down: bfloat16 [5632, 2048], P('fsdp'), may hold values from -0.15625 to 0.15625
- cotangent: bfloat16 [4, 1280, 2048], P('fsdp', 'seq'), may hold values from -6 to 6
Outputs:
- output: bfloat16 [4, 1280, 2048], P('fsdp', 'seq')
- grad_hidden: bfloat16 [4, 1280, 2048], P('fsdp', 'seq')
- grad_w_input: float32 [2048, 2048], P('seq', 'fsdp')
- grad_w_forget: float32 [2048, 2048], P('seq', 'fsdp')
- grad_w_gate_out: float32 [2048, 2048], P('seq', 'fsdp')
- grad_w_output: float32 [2048, 2048], P('fsdp', 'seq')
- grad_norm_gain: float32 [2048], replicated
- grad_gate_gain: float32 [2048], replicated
- grad_glu_gain: float32 [2048], replicated
- grad_lower_table: float32 [24, 2048], replicated
- grad_glu_gate: float32 [2048, 5632], P('seq', 'fsdp')
- grad_glu_up: float32 [2048, 5632], P('seq', 'fsdp')
- grad_glu_down: float32 [5632, 2048], P('fsdp', 'seq')
Inputs may be any that keep to these rules, and one draw needn't show every extreme that they name: Each row holds the lengths of one group's 4 sequences; they sum to 1280 and the largest is 1024.
All inputs are finite; a program needn't handle non-finite values.
Results may differ from a plain program's by a relative error of at most 0.017.
Values may be sent and summed in bfloat16 or wider, within the bound.
A program may use at most 256 MiB of HBM per device.

v0:
```python
import jax
import jax.numpy as jnp
from jax import lax
from jax.sharding import PartitionSpec as P

LAYER = 12


epsilon = 1e-06


def combine(earlier, later):
    return (earlier[0] * later[0], later[0] * earlier[1] + later[1])


def lower_bound(table):
    soft = jax.nn.softmax(table, axis=0)
    totals = jnp.cumsum(soft, axis=0)
    return totals[LAYER] - totals[0]


def silu_slope(value, sigma):
    return sigma * (1.0 + value * (1.0 - sigma))


def mixer_rows(normed):
    return lax.all_gather(normed, "fsdp", axis=0, tiled=True)


def regroup_pairs(pairs):
    return lax.all_to_all(pairs, "seq", split_axis=0, concat_axis=0, tiled=True)


def regroup_states(states):
    return lax.all_to_all(states, "seq", split_axis=0, concat_axis=0, tiled=True)


def row_sums(partial_value):
    return lax.psum(partial_value, "fsdp")


def per_device(
    hidden,
    lengths,
    w_input,
    w_forget,
    w_gate_out,
    w_output,
    norm_gain,
    gate_gain,
    glu_gain,
    lower_table,
    w_glu_gate,
    w_glu_up,
    w_glu_down,
    cotangent,
):
    n_seq = lax.axis_size("seq")
    n_fsdp = lax.axis_size("fsdp")
    seq_index = lax.axis_index("seq")
    fsdp_index = lax.axis_index("fsdp")
    width = hidden.shape[2]
    tok_rows = hidden.shape[1]
    chans = w_input.shape[1]
    items = width // n_seq
    per_group = chans // items
    group_len = n_seq * tok_rows
    units = w_glu_gate.shape[1]
    hidden_f = hidden[0].astype(jnp.float32)
    scale_one = lax.rsqrt(jnp.mean(hidden_f * hidden_f, -1, keepdims=True) + epsilon)
    normed = (hidden_f * scale_one * norm_gain).astype(jnp.bfloat16)[None]
    normed_all = mixer_rows(normed)
    w_three = jnp.concatenate([w_input, w_forget, w_gate_out], 1)
    projected = jnp.einsum("gtd,dc->gtc", normed_all, w_three, preferred_element_type=jnp.float32)
    pair_tokens = projected[:, :, : 2 * chans].astype(jnp.bfloat16)
    pair_tokens = pair_tokens.reshape(n_fsdp, tok_rows, 2, per_group, items).transpose(
        0, 3, 1, 2, 4
    )
    pair_tokens = pair_tokens.reshape(n_seq, tok_rows, 2, items)
    gate_raw = projected[:, :, 2 * chans :]
    pair_time = regroup_pairs(pair_tokens).reshape(group_len, 2, items).astype(jnp.float32)
    in_raw = pair_time[:, 0, :]
    forget_raw = pair_time[:, 1, :]
    group_id = seq_index // per_group
    channel_start = fsdp_index * chans + seq_index % per_group * items
    group_lengths = lax.dynamic_slice(lengths, (group_id, 0), (1, lengths.shape[1]))[0]
    seq_starts = jnp.cumsum(group_lengths) - group_lengths
    places = jnp.arange(group_len, dtype=jnp.int32)
    keep = jnp.where(jnp.any(places[:, None] == seq_starts[None, :], axis=1), 0.0, 1.0).astype(
        jnp.float32
    )[:, None]
    bounds_full = lower_bound(lower_table)
    bounds = lax.dynamic_slice_in_dim(bounds_full, channel_start, items)
    sigma_f = jax.nn.sigmoid(forget_raw)
    forget = bounds + (1.0 - bounds) * sigma_f
    sigma_i = jax.nn.sigmoid(in_raw)
    silu_in = in_raw * sigma_i
    inflow = silu_in * (1.0 - forget)
    carry_mul = forget * keep
    states = lax.associative_scan(combine, (carry_mul, inflow), axis=0)[1]
    state_tokens = regroup_states(states.astype(jnp.bfloat16).reshape(n_seq, tok_rows, items))
    state_tokens = state_tokens.reshape(n_fsdp, per_group, tok_rows, items).transpose(0, 2, 1, 3)
    state_tokens = state_tokens.reshape(n_fsdp, tok_rows, chans).astype(jnp.float32)
    square_rows = row_sums(jnp.sum(state_tokens * state_tokens, -1))
    state_scale = lax.rsqrt(square_rows / width + epsilon)[:, :, None]
    gain_slice = lax.dynamic_slice_in_dim(gate_gain, fsdp_index * chans, chans)
    sigma_g = jax.nn.sigmoid(gate_raw)
    silu_gate = gate_raw * sigma_g
    scaled_state = state_tokens * state_scale
    out_gate = (scaled_state * gain_slice * silu_gate).astype(jnp.bfloat16)
    block = out_gate
    mixed = lax.psum_scatter(
        jnp.einsum("gtc,cd->gtd", block, w_output, preferred_element_type=jnp.float32),
        "fsdp",
        scatter_dimension=0,
        tiled=True,
    )[0]
    middle = hidden_f + mixed
    scale_two = lax.rsqrt(jnp.mean(middle * middle, -1, keepdims=True) + epsilon)
    normed_two = (middle * scale_two * glu_gain).astype(jnp.bfloat16)[None]
    normed_two_all, cotangent_all = (
        lax.all_gather(normed_two, "fsdp", axis=0, tiled=True),
        lax.all_gather(cotangent, "fsdp", axis=0, tiled=True),
    )
    w_pair = jnp.concatenate([w_glu_gate, w_glu_up], 1)
    gate_up = jnp.einsum("gtd,df->gtf", normed_two_all, w_pair, preferred_element_type=jnp.float32)
    gate_val = gate_up[:, :, :units]
    up_val = gate_up[:, :, units:]
    sigma_u = jax.nn.sigmoid(gate_val)
    silu_u = gate_val * sigma_u
    activity = (silu_u * up_val).astype(jnp.bfloat16)
    block = activity
    glu_result = lax.psum_scatter(
        jnp.einsum("gtf,fd->gtd", block, w_glu_down, preferred_element_type=jnp.float32).astype(
            jnp.bfloat16
        ),
        "fsdp",
        scatter_dimension=0,
        tiled=True,
    ).astype(jnp.float32)[0]
    output = (middle + glu_result).astype(jnp.bfloat16)[None]
    cotangent_f = cotangent[0].astype(jnp.float32)
    d_glu_down = jnp.einsum(
        "gtf,gtd->fd", activity, cotangent_all, preferred_element_type=jnp.float32
    )
    d_act = jnp.einsum("gtd,fd->gtf", cotangent_all, w_glu_down, preferred_element_type=jnp.float32)
    d_gate = d_act * up_val * silu_slope(gate_val, sigma_u)
    d_up = d_act * silu_u
    d_gate_up = jnp.concatenate([d_gate, d_up], -1).astype(jnp.bfloat16)
    d_w_pair = jnp.einsum(
        "gtd,gtf->df", normed_two_all, d_gate_up, preferred_element_type=jnp.float32
    )
    block = d_gate_up
    d_normed_two = lax.psum_scatter(
        jnp.einsum("gtf,df->gtd", block, w_pair, preferred_element_type=jnp.float32),
        "fsdp",
        scatter_dimension=0,
        tiled=True,
    )[0]
    scaled_two = glu_gain * d_normed_two
    d_middle = (
        cotangent_f
        + scale_two * scaled_two
        - middle * scale_two**3 * jnp.mean(scaled_two * middle, -1, keepdims=True)
    )
    d_glu_gain = jnp.sum(d_normed_two * middle * scale_two, 0)
    d_mixed = d_middle.astype(jnp.bfloat16)[None]
    d_mixed_all = lax.all_gather(d_mixed, "fsdp", axis=0, tiled=True)
    d_w_output = jnp.einsum(
        "gtc,gtd->cd", out_gate, d_mixed_all, preferred_element_type=jnp.float32
    )
    d_out = jnp.einsum("gtd,cd->gtc", d_mixed_all, w_output, preferred_element_type=jnp.float32)
    d_gain_slice = jnp.sum(d_out * scaled_state * silu_gate, (0, 1))
    d_scaled = d_out * gain_slice * silu_gate
    d_gate_raw = (d_out * scaled_state * gain_slice * silu_slope(gate_raw, sigma_g)).astype(
        jnp.bfloat16
    )
    dot_rows = row_sums(jnp.sum(d_scaled * state_tokens, -1))
    d_state = (
        state_scale * d_scaled - state_tokens * state_scale**3 * (dot_rows / width)[:, :, None]
    )
    d_state = (
        d_state.astype(jnp.bfloat16)
        .reshape(n_fsdp, tok_rows, per_group, items)
        .transpose(0, 2, 1, 3)
    )
    d_state_time = (
        regroup_states(d_state.reshape(n_seq, tok_rows, items))
        .reshape(group_len, items)
        .astype(jnp.float32)
    )
    next_mul = jnp.concatenate([carry_mul[1:], jnp.zeros((1, items), jnp.float32)], 0)
    accumulated = lax.associative_scan(combine, (next_mul, d_state_time), reverse=True, axis=0)[1]
    states_prev = jnp.concatenate([jnp.zeros((1, items), jnp.float32), states[:-1]], 0)
    d_forget = accumulated * states_prev * keep - accumulated * silu_in
    d_in_raw = accumulated * (1.0 - forget) * silu_slope(in_raw, sigma_i)
    d_forget_raw = d_forget * (1.0 - bounds) * sigma_f * (1.0 - sigma_f)
    d_bounds = jnp.sum(d_forget * (1.0 - sigma_f), 0)
    d_pairs = (
        jnp.stack([d_in_raw, d_forget_raw], 1)
        .astype(jnp.bfloat16)
        .reshape(n_seq, tok_rows, 2, items)
    )
    d_pair_tokens = (
        regroup_pairs(d_pairs)
        .reshape(n_fsdp, per_group, tok_rows, 2, items)
        .transpose(0, 2, 3, 1, 4)
    )
    d_pair_tokens = d_pair_tokens.reshape(n_fsdp, tok_rows, 2 * chans)
    d_projected = jnp.concatenate([d_pair_tokens, d_gate_raw], -1)
    normed_back = mixer_rows(normed)
    d_w_three = jnp.einsum(
        "gtd,gtc->dc", normed_back, d_projected, preferred_element_type=jnp.float32
    )
    block = d_projected
    d_normed = lax.psum_scatter(
        jnp.einsum("gtc,dc->gtd", block, w_three, preferred_element_type=jnp.float32).astype(
            jnp.bfloat16
        ),
        "fsdp",
        scatter_dimension=0,
        tiled=True,
    ).astype(jnp.float32)[0]
    scaled_one = norm_gain * d_normed
    d_hidden = (
        d_middle
        + scale_one * scaled_one
        - hidden_f * scale_one**3 * jnp.mean(scaled_one * hidden_f, -1, keepdims=True)
    )
    d_norm_gain = jnp.sum(d_normed * hidden_f * scale_one, 0)
    d_gain_full = lax.dynamic_update_slice(
        jnp.zeros((width,), jnp.float32), d_gain_slice, (fsdp_index * chans,)
    )
    d_bounds_full = lax.dynamic_update_slice(
        jnp.zeros((width,), jnp.float32), d_bounds, (channel_start,)
    )
    total_norm, total_glu, total_gate, total_bounds = lax.psum(
        (d_norm_gain, d_glu_gain, d_gain_full, d_bounds_full), ("seq", "fsdp")
    )
    bounds_again, bounds_pull = jax.vjp(lower_bound, lower_table)
    d_table = bounds_pull(total_bounds)[0]
    grads_owned = (
        lax.psum_scatter(
            d_w_three[:, :chans].astype(jnp.bfloat16), "seq", scatter_dimension=0, tiled=True
        ).astype(jnp.float32),
        lax.psum_scatter(
            d_w_three[:, chans : 2 * chans].astype(jnp.bfloat16),
            "seq",
            scatter_dimension=0,
            tiled=True,
        ).astype(jnp.float32),
        lax.psum_scatter(
            d_w_three[:, 2 * chans :].astype(jnp.bfloat16), "seq", scatter_dimension=0, tiled=True
        ).astype(jnp.float32),
        lax.psum_scatter(
            d_w_output.astype(jnp.bfloat16), "seq", scatter_dimension=1, tiled=True
        ).astype(jnp.float32),
        lax.psum_scatter(
            d_w_pair[:, :units].astype(jnp.bfloat16), "seq", scatter_dimension=0, tiled=True
        ).astype(jnp.float32),
        lax.psum_scatter(
            d_w_pair[:, units:].astype(jnp.bfloat16), "seq", scatter_dimension=0, tiled=True
        ).astype(jnp.float32),
        lax.psum_scatter(
            d_glu_down.astype(jnp.bfloat16), "seq", scatter_dimension=1, tiled=True
        ).astype(jnp.float32),
    )
    return (
        output,
        d_hidden.astype(jnp.bfloat16)[None],
        grads_owned[0],
        grads_owned[1],
        grads_owned[2],
        grads_owned[3],
        total_norm,
        total_gate,
        total_glu,
        d_table,
        grads_owned[4],
        grads_owned[5],
        grads_owned[6],
    )


def solution(mesh):
    placed = (
        P("fsdp", "seq", None),
        P(),
        P(None, "fsdp"),
        P(None, "fsdp"),
        P(None, "fsdp"),
        P("fsdp", None),
        P(),
        P(),
        P(),
        P(),
        P(None, "fsdp"),
        P(None, "fsdp"),
        P("fsdp", None),
        P("fsdp", "seq", None),
    )
    return jax.shard_map(
        per_device,
        mesh=mesh,
        in_specs=placed,
        out_specs=(
            P("fsdp", "seq", None),
            P("fsdp", "seq", None),
            P("seq", "fsdp"),
            P("seq", "fsdp"),
            P("seq", "fsdp"),
            P("fsdp", "seq"),
            P(),
            P(),
            P(),
            P(),
            P("seq", "fsdp"),
            P("seq", "fsdp"),
            P("fsdp", "seq"),
        ),
        check_vma=False,
    )
```

profile of v0, /device:TPU:8, one launch (start us, length us, event | category | flops | bytes accessed | tf_op | source)
XLA Modules:
  0.0 995.2 jit_solution(5606895325581948570)
XLA Ops:
  11.5 41.0 %all-gather.5.cloned.1.call-done = bf16[4,160,2048]{2,1,0:T(8,128)(2,1)} async-done(((bf16[1,160,2048]{2,1,0:T(8,128)(2,1)}), bf16[4,160,2048]{2,1,0:T(8,128)(2,1)}) %all-gather.5.cloned.1.call-update) | async-done | bytes 2621456 | tf_op jit(solution)/shard_map/all_gather | solution.py:27
  52.4 7.8 fusion.8
  76.4 28.0 %all-to-all-done = bf16[8,160,2,256]{3,1,2,0:T(8,128)(2,1)} async-done(((bf16[8,160,2,256]{3,1,2,0:T(8,128)(2,1)}), bf16[8,160,2,256]{3,1,2,0:T(8,128)(2,1)}, u32[]{:S(2)}, u32[]{:S(2)}) %all-to-all-start) | async-done | bytes 1310752 | tf_op jit(solution)/shard_map/all_to_all | solution.py:31
  165.5 7.0 all-to-all-start.1
  173.3 13.9 %all-to-all-done.1 = bf16[8,160,256]{2,1,0:T(8,128)(2,1)S(1)} async-done(((bf16[8,160,256]{2,1,0:T(8,128)(2,1)}), bf16[8,160,256]{2,1,0:T(8,128)(2,1)S(1)}, u32[]{:S(2)}, u32[]{:S(2)}) %all-to-all-start.1) | async-done | bytes 655392 | tf_op jit(solution)/shard_map/all_to_all | solution.py:35
  187.6 9.1 psum.42
  203.1 62.4 %reduce-scatter.34.cloned.1.call-done = f32[1,160,2048]{2,1,0:T(8,128)} async-done(((f32[4,160,2048]{2,1,0:T(8,128)}), f32[1,160,2048]{2,1,0:T(8,128)}) %reduce-scatter.34.cloned.1.call-update) | async-done | bytes 1310736
  269.0 39.1 %all-gather.7.cloned.1.call-done = bf16[4,160,2048]{2,1,0:T(8,128)(2,1)} async-done(((bf16[1,160,2048]{2,1,0:T(8,128)(2,1)}), bf16[4,160,2048]{2,1,0:T(8,128)(2,1)}) %all-gather.7.cloned.1.call-update) | async-done | bytes 2621456 | tf_op jit(solution)/shard_map/all_gather | solution.py:122
  308.1 15.5 %fusion.1 = f32[4,160,2816]{2,1,0:T(8,128)} fusion(bf16[4,160,2048]{2,1,0:T(8,128)(2,1)} %all-gather.7.cloned.1.call-done, bf16[2048,1408]{1,0:T(8,128)(2,1)} %param.25, bf16[2048,1408]{1,0:T(8,128)(2,1)} %param.24), kind=kOutput, calls=%fused_computation.5 | convolution fusion | flops 7405043712 | bytes 21364736 | tf_op jit(solution)/shard_map/gtd,df->gtf/dot_general | solution.py:126
  323.6 25.8 %all-gather.9.cloned.1.call-done = bf16[4,160,2048]{2,1,0:T(8,128)(2,1)} async-done(((bf16[1,160,2048]{2,1,0:T(8,128)(2,1)}), bf16[4,160,2048]{2,1,0:T(8,128)(2,1)}) %all-gather.9.cloned.1.call-update) | async-done | bytes 2621456 | tf_op jit(solution)/shard_map/all_gather | solution.py:123
  349.5 12.1 %multiply_convert_fusion.1 = (bf16[4,160,1408]{2,1,0:T(8,128)(2,1)S(1)}, bf16[4,160,1408]{2,1,0:T(8,128)(2,1)S(1)}, bf16[4,160,1408]{2,1,0:T(8,128)(2,1)}) fusion(f32[4,160,2816]{2,1,0:T(8,128)} %fusion.1, bf16[4,160,2048]{2,1,0:T(8,128)(2,1)} %all-gather.9.cloned.1.call-done, bf16[1408,2048]{1,0:T(8,128)(2,1)} %param.26), kind=kOutput, calls=%fused_computation.14 | convolution fusion | flops 3704504320 | bytes 21004288 | tf_op jit(solution)/shard_map/gtd,fd->gtf/dot_general | solution.py:146
  363.4 12.5 %fusion = f32[4,160,2048]{2,1,0:T(8,128)} fusion(bf16[2048,1408]{1,0:T(8,128)(2,1)} %param.25, bf16[2048,1408]{1,0:T(8,128)(2,1)} %param.24, bf16[4,160,1408]{2,1,0:T(8,128)(2,1)S(1)} %get-tuple-element.30, bf16[4,160,1408]{2,1,0:T(8,128)(2,1)S(1)} %get-tuple-element.29), kind=kOutput, calls=%fused_computation.4 | convolution fusion | flops 7412252672 | bytes 20381696 | tf_op jit(solution)/shard_map/gtf,df->gtd/dot_general | solution.py:155
  376.0 8.9 fusion.9
  385.0 52.5 %reduce-scatter.38.cloned.1.call-done = f32[1,160,2048]{2,1,0:T(8,128)} async-done(((f32[4,160,2048]{2,1,0:T(8,128)}), f32[1,160,2048]{2,1,0:T(8,128)}) %reduce-scatter.38.cloned.1.call-update) | async-done | bytes 1310736
  440.2 39.8 %reduce-scatter.36.cloned.1.call-done = bf16[1,160,2048]{2,1,0:T(8,128)(2,1)} async-done(((bf16[4,160,2048]{2,1,0:T(8,128)(2,1)}), bf16[1,160,2048]{2,1,0:T(8,128)(2,1)}) %reduce-scatter.36.cloned.1.call-update) | async-done | bytes 655376
  484.2 9.4 bitcast_convert_fusion.2
  493.6 14.5 %bitcast_convert_fusion = bf16[2048,2816]{1,0:T(8,128)(2,1)} fusion(bf16[4,160,2048]{2,1,0:T(8,128)(2,1)} %all-gather.7.cloned.1.call-done, bf16[4,160,1408]{2,1,0:T(8,128)(2,1)} %copy-done.52, bf16[4,160,1408]{2,1,0:T(8,128)(2,1)} %copy-done.51), kind=kOutput, calls=%fused_computation | convolution fusion | flops 7394951168 | bytes 17760256 | tf_op jit(solution)/shard_map/gtd,gtf->df/dot_general | solution.py:150
  508.2 9.4 fusion.72
  539.5 6.1 slice.615
  551.5 6.1 multiply_reduce_fusion.1
  557.6 9.2 psum.43
  583.1 16.7 %all-to-all-done.2 = bf16[8,160,256]{2,1,0:T(8,128)(2,1)} async-done(((bf16[8,160,256]{2,1,0:T(8,128)(2,1)}), bf16[8,160,256]{2,1,0:T(8,128)(2,1)}, u32[]{:S(2)}, u32[]{:S(2)}) %all-to-all-start.2) | async-done | bytes 655392 | tf_op jit(solution)/shard_map/all_to_all | solution.py:35
  614.6 5.9 slice.619
  710.9 10.7 %rev.2 = f32[1280,256]{1,0:T(8,128)} reverse(f32[1280,256]{1,0:T(8,128)} %add.472), dimensions={0} | reverse | bytes 2621440 | tf_op jit(solution)/shard_map/rev | solution.py:193
  725.8 48.9 %all_to_all.20 = bf16[8,160,2,256]{3,1,2,0:T(8,128)(2,1)S(1)} all-to-all(bf16[8,160,2,256]{3,1,2,0:T(8,128)(2,1)S(1)} %pad_maximum_fusion.4), channel_id=1, replica_groups=mesh['seq'=8,'fsdp'=4] {'seq'}, dimensions={0} | all-to-all | bytes 2621440 | tf_op jit(solution)/shard_map/all_to_all | solution.py:31
  781.4 7.1 bitcast_convert_fusion.1
  792.8 8.1 fusion.12
  810.8 13.3 %reduce-scatter.20.cloned.1.call-done = bf16[256,512]{1,0:T(8,128)(2,1)} async-done(((bf16[2048,512]{1,0:T(8,128)(2,1)}), bf16[256,512]{1,0:T(8,128)(2,1)}) %reduce-scatter.20.cloned.1.call-update) | async-done | bytes 262160 | tf_op jit(solution)/shard_map/reduce_scatter | solution.py:243
  825.9 34.9 %reduce-scatter.22.cloned.1.call-done = bf16[256,512]{1,0:T(8,128)(2,1)} async-done(((bf16[2048,512]{1,0:T(8,128)(2,1)}), bf16[256,512]{1,0:T(8,128)(2,1)}) %reduce-scatter.22.cloned.1.call-update) | async-done | bytes 262160 | tf_op jit(solution)/shard_map/reduce_scatter | solution.py:246
  862.6 34.9 %reduce-scatter.24.cloned.1.call-done = bf16[256,512]{1,0:T(8,128)(2,1)} async-done(((bf16[2048,512]{1,0:T(8,128)(2,1)}), bf16[256,512]{1,0:T(8,128)(2,1)}) %reduce-scatter.24.cloned.1.call-update) | async-done | bytes 262160 | tf_op jit(solution)/shard_map/reduce_scatter | solution.py:252
  899.4 42.8 %reduce-scatter.40.cloned.1.call-done = bf16[1,160,2048]{2,1,0:T(8,128)(2,1)} async-done(((bf16[4,160,2048]{2,1,0:T(8,128)(2,1)}), bf16[1,160,2048]{2,1,0:T(8,128)(2,1)}) %reduce-scatter.40.cloned.1.call-update) | async-done | bytes 655376
  943.7 40.0 %all-reduce.48 = (f32[2048]{0:T(1024)}, f32[2048]{0:T(1024)}, f32[2048]{0:T(1024)}, f32[2048]{0:T(1024)S(1)}) all-reduce(f32[2048]{0:T(1024)S(1)} %get-tuple-element.17, f32[2048]{0:T(1024)S(1)} %dynamic_update_slice.6, f32[2048]{0:T(1024)S(1)} %copy-done.37, ...), channel_id=1, replica_groups=mesh['seq'=8,'fsdp'=4] {'seq','fsdp'}, use_global_device_ids=true, to_apply=%region_23.24 | all-reduce | flops 8192 | bytes 65536 | tf_op jit(solution)/shard_map/psum | solution.py:237
  (453 shorter events, 285.8 us)
Async XLA Ops:
  7.2 192.0 %copy-start = (bf16[512,2048]{1,0:T(8,128)(2,1)S(1)}, bf16[512,2048]{1,0:T(8,128)(2,1)}, u32[]{:S(2)}) copy-start(bf16[512,2048]{1,0:T(8,128)(2,1)} %param.19) | copy-start | bytes 6291460
  7.2 45.2 %all-gather.5.cloned.1.call-start = ((), (), s32[]{:S(2)}) async-start(), calls=%async_computation.15 | async-start | bytes 3276800 | tf_op jit(solution)/shard_map/all_gather | solution.py:27
  9.3 51.0 %copy-start.42 = (f32[160]{0:T(256)}, f32[160]{0:T(256)S(1)}, u32[]{:S(2)}) copy-start(f32[160]{0:T(256)S(1)} %get-tuple-element.88) | copy-start | bytes 1924
  70.4 34.0 %all-to-all-start = ((bf16[8,160,2,256]{3,1,2,0:T(8,128)(2,1)}), bf16[8,160,2,256]{3,1,2,0:T(8,128)(2,1)}, u32[]{:S(2)}, u32[]{:S(2)}) async-start(bf16[8,160,2,256]{3,1,2,0:T(8,128)(2,1)} %bitcast.163), calls=%async_computation | async-start | bytes 2621440 | tf_op jit(solution)/shard_map/all_to_all | solution.py:31
  75.9 30.1 %copy-start.28 = (f32[2048]{0:T(1024)}, f32[2048]{0:T(1024)S(1)}, u32[]{:S(2)}) copy-start(f32[2048]{0:T(1024)S(1)} %reduce_max.8) | copy-start | bytes 24580
  75.9 30.1 %copy-start.30 = (f32[2048]{0:T(1024)}, f32[2048]{0:T(1024)S(1)}, u32[]{:S(2)}) copy-start(f32[2048]{0:T(1024)S(1)} %fusion.51) | copy-start | bytes 24580
  76.2 29.8 %copy-start.40 = (f32[1,256]{1,0:T(1,128)}, f32[1,256]{1,0:T(1,128)S(1)}, u32[]{:S(2)}) copy-start(f32[1,256]{1,0:T(1,128)S(1)} %dynamic-slice_subtract_fusion) | copy-start | bytes 3076
  76.3 29.7 %copy-start.38 = (f32[256]{0:T(256)}, f32[256]{0:T(256)S(1)}, u32[]{:S(2)}) copy-start(f32[256]{0:T(256)S(1)} %broadcast_subtract_fusion) | copy-start | bytes 3076
  165.5 21.7 %all-to-all-start.1 = ((bf16[8,160,256]{2,1,0:T(8,128)(2,1)}), bf16[8,160,256]{2,1,0:T(8,128)(2,1)S(1)}, u32[]{:S(2)}, u32[]{:S(2)}) async-start(bf16[8,160,256]{2,1,0:T(8,128)(2,1)} %bitcast.9), calls=%async_computation.1 | async-start | bytes 1310720 | tf_op jit(solution)/shard_map/all_to_all | solution.py:35
  172.5 93.0 %reduce-scatter.34.cloned.1.call-start = ((), (), s32[]{:S(2)}) async-start(), calls=%async_computation.26 | async-start | bytes 6553600
  203.0 62.5 %copy-start.1 = (bf16[1,160,2048]{2,1,0:T(8,128)(2,1)S(1)}, bf16[1,160,2048]{2,1,0:T(8,128)(2,1)}, u32[]{:S(2)}) copy-start(bf16[1,160,2048]{2,1,0:T(8,128)(2,1)} %param.14) | copy-start | bytes 1966084
  203.1 64.2 %copy-start.33 = (f32[2048]{0:T(1024)S(1)}, f32[2048]{0:T(1024)}, u32[]{:S(2)}) copy-start(f32[2048]{0:T(1024)} %param.22) | copy-start | bytes 24580
  203.1 105.0 %all-gather.7.cloned.1.call-start = ((), (), s32[]{:S(2)}) async-start(), calls=%async_computation.16 | async-start | bytes 3276800 | tf_op jit(solution)/shard_map/all_gather | solution.py:122
  268.3 81.1 %all-gather.9.cloned.1.call-start = ((), (), s32[]{:S(2)}) async-start(), calls=%async_computation.17 | async-start | bytes 3276800 | tf_op jit(solution)/shard_map/all_gather | solution.py:123
  268.9 168.6 %reduce-scatter.38.cloned.1.call-start = ((), (), s32[]{:S(2)}) async-start(), calls=%async_computation.28 | async-start | bytes 6553600
  376.0 104.0 %reduce-scatter.36.cloned.1.call-start = ((), (), s32[]{:S(2)}) async-start(), calls=%async_computation.27 | async-start | bytes 3276800
  385.0 166.5 %all-gather.11.cloned.1.call-start = ((), (), s32[]{:S(2)}) async-start(), calls=%async_computation.18 | async-start | bytes 3276800 | tf_op jit(solution)/shard_map/all_gather | solution.py:168
  484.1 317.5 %reduce-scatter.32.cloned.1.call-start = ((), (), s32[]{:S(2)}) async-start(), calls=%async_computation.25 | async-start | bytes 6488064 | tf_op jit(solution)/shard_map/reduce_scatter | solution.py:264
  493.6 310.3 %reduce-scatter.28.cloned.1.call-start = ((), (), s32[]{:S(2)}) async-start(), calls=%async_computation.23 | async-start | bytes 6488064 | tf_op jit(solution)/shard_map/reduce_scatter | solution.py:258
  517.6 288.6 %reduce-scatter.30.cloned.1.call-start = ((), (), s32[]{:S(2)}) async-start(), calls=%async_computation.24 | async-start | bytes 6488064 | tf_op jit(solution)/shard_map/reduce_scatter | solution.py:261
  571.6 28.3 %all-to-all-start.2 = ((bf16[8,160,256]{2,1,0:T(8,128)(2,1)}), bf16[8,160,256]{2,1,0:T(8,128)(2,1)}, u32[]{:S(2)}, u32[]{:S(2)}) async-start(bf16[8,160,256]{2,1,0:T(8,128)(2,1)} %bitcast.166), calls=%async_computation.2 | async-start | bytes 1310720 | tf_op jit(solution)/shard_map/all_to_all | solution.py:35
  576.7 232.3 %reduce-scatter.26.cloned.1.call-start = ((), (), s32[]{:S(2)}) async-start(), calls=%async_computation.22 | async-start | bytes 2359296 | tf_op jit(solution)/shard_map/reduce_scatter | solution.py:255
  583.0 241.0 %reduce-scatter.20.cloned.1.call-start = ((), (), s32[]{:S(2)}) async-start(), calls=%async_computation.19 | async-start | bytes 2359296 | tf_op jit(solution)/shard_map/reduce_scatter | solution.py:243
  791.4 69.4 %reduce-scatter.22.cloned.1.call-start = ((), (), s32[]{:S(2)}) async-start(), calls=%async_computation.20 | async-start | bytes 2359296 | tf_op jit(solution)/shard_map/reduce_scatter | solution.py:246
  792.1 105.4 %reduce-scatter.24.cloned.1.call-start = ((), (), s32[]{:S(2)}) async-start(), calls=%async_computation.21 | async-start | bytes 2359296 | tf_op jit(solution)/shard_map/reduce_scatter | solution.py:252
  792.7 149.5 %reduce-scatter.40.cloned.1.call-start = ((), (), s32[]{:S(2)}) async-start(), calls=%async_computation.29 | async-start | bytes 3276800
  810.8 131.4 %copy-start.36 = (f32[2048]{0:T(1024)S(1)}, f32[2048]{0:T(1024)}, u32[]{:S(2)}) copy-start(f32[2048]{0:T(1024)} %param.20) | copy-start | bytes 24580
  810.8 131.4 %copy-start.43 = (f32[160]{0:T(256)S(1)}, f32[160]{0:T(256)}, u32[]{:S(2)}) copy-start(f32[160]{0:T(256)} %copy-done.42) | copy-start | bytes 1924
  825.9 117.8 %copy-start.37 = (f32[2048]{0:T(1024)S(1)}, f32[2048]{0:T(1024)}, u32[]{:S(2)}) copy-start(f32[2048]{0:T(1024)} %get-tuple-element.15) | copy-start | bytes 24580
  862.6 121.8 %copy-start.9 = (f32[24,2048]{1,0:T(8,128)S(1)}, f32[24,2048]{1,0:T(8,128)}, u32[]{:S(2)}) copy-start(f32[24,2048]{1,0:T(8,128)} %param.23) | copy-start | bytes 589828
  862.6 121.9 %copy-start.29 = (f32[2048]{0:T(1024)S(1)}, f32[2048]{0:T(1024)}, u32[]{:S(2)}) copy-start(f32[2048]{0:T(1024)} %copy-done.28) | copy-start | bytes 24580
  899.4 85.9 %copy-start.44 = (f32[160]{0:T(256)S(1)}, f32[160]{0:T(256)}, u32[]{:S(2)}) copy-start(f32[160]{0:T(256)} %get-tuple-element.87) | copy-start | bytes 1924
  (39 other events, 205.0 us)
Sparse Core Ops, SparseCore 0:
  11.6 40.7 all-gather.4
  203.2 62.3 reduce-scatter.33
  268.4 39.6 all-gather.6
  309.8 39.6 all-gather.8
  376.1 61.4 reduce-scatter.37
  440.4 39.5 reduce-scatter.35
  484.2 39.6 all-gather.10
  526.2 70.5 reduce-scatter.31
  599.1 67.7 reduce-scatter.27
  669.1 63.2 reduce-scatter.29
  734.6 49.9 reduce-scatter.25
  791.5 32.5 reduce-scatter.19
  826.4 34.3 reduce-scatter.21
  863.0 34.5 reduce-scatter.23
  900.4 41.7 reduce-scatter.39
where the time goes:
time: 1010 us; the launch traced here: 995 us
  waiting for transfers between devices  448 us (44%)
  local copies, waits for them, and re-layouts  208 us (21%)
  matrix products  109 us (11%)
  blocking collectives  107 us (11%)
  other arithmetic  89.3 us (9%)
  starting transfers between devices  18 us (2%)
  between operations  15.6 us (2%)
    unnamed x19, waiting for transfers between devices  200 us
    slice x69, local copies, waits for them, and re-layouts, per_device(): lax.associative_scan(combine, (next_mul, d_state_time), reverse=True, axi...  97.9 us
    all_to_all x1, blocking collectives, regroup_pairs(): return lax.all_to_all(pairs, 'seq', split_axis=0, concat_axis=0, tiled=True)  48.9 us
    all_gather x1, waiting for transfers between devices, mixer_rows(): return lax.all_gather(normed, 'fsdp', axis=0, tiled=True)  41 us
    psum x1, blocking collectives, per_device(): lax.psum((d_norm_gain, d_glu_gain, d_gain_full, d_bounds_full), ('seq', '...  40 us
    all_gather x1, waiting for transfers between devices, per_device(): lax.all_gather(normed_two, 'fsdp', axis=0, tiled=True)  39.1 us
    slice x63, local copies, waits for them, and re-layouts, per_device(): states = lax.associative_scan(combine, (carry_mul, inflow), axis=0)[1]  38 us
    reduce_scatter x1, waiting for transfers between devices, per_device(): lax.psum_scatter(d_w_three[:, 2 * chans:].astype(jnp.bfloat16), 'seq', sc...  34.9 us
  transfers between devices with their start and end apart: 18, of which 13 were waited for; matrix products, arithmetic and copies ran while one was open for 28% of the time, Pallas kernels for 0%

commit v1 on v0

v1 whole, which is shorter than its diff:
```python
import functools

import jax
import jax.numpy as jnp
from jax import lax
from jax.experimental import pallas as pl
from jax.experimental.pallas import tpu as pltpu
from jax.sharding import PartitionSpec as P

LAYER = 12
MESH = pl.DeviceIdType.MESH
F32 = jnp.float32
BF16 = jnp.bfloat16

epsilon = 1e-06

VMEM = pl.BlockSpec(memory_space=pltpu.VMEM)
ANY = pl.BlockSpec(memory_space=pl.ANY)


def lower_bound(table):
    soft = jax.nn.softmax(table, axis=0)
    totals = jnp.cumsum(soft, axis=0)
    return totals[LAYER] - totals[0]


def silu_slope(value, sigma):
    return sigma * (1.0 + value * (1.0 - sigma))


def params(collective_id):
    return pltpu.CompilerParams(
        collective_id=collective_id, has_side_effects=True, vmem_limit_bytes=56 << 20
    )


def round_up(value, unit):
    return -(-value // unit) * unit


def plane():
    s = lax.axis_index("seq")
    f = lax.axis_index("fsdp")
    y, x = f // 2, f % 2
    fx = y * 2 + (1 - x)
    fy = (1 - y) * 2 + x
    fd = (1 - y) * 2 + (1 - x)
    return s, f, fx, fy, fd


def enter(devices):
    barrier = pltpu.get_barrier_semaphore()
    for device in devices:
        pl.semaphore_signal(barrier, inc=1, device_id=device, device_id_type=MESH)
    pl.semaphore_wait(barrier, len(devices))


def remote(src, dst, send, recv, device):
    return pltpu.make_async_remote_copy(
        src_ref=src,
        dst_ref=dst,
        send_sem=send,
        recv_sem=recv,
        device_id=device,
        device_id_type=MESH,
    )


def gather_kernel(x, small, out, out_small, local_sem, send, recv):
    s, f, fx, fy, fd = plane()
    half = x.shape[0] // 2
    enter([(s, fx), (s, fy), (s, fd)])
    top, bottom = pl.ds(0, half), pl.ds(half, half)
    own = [
        remote(x.at[top], out.at[f, top], send.at[0], recv.at[0], (s, fx)),
        remote(x.at[bottom], out.at[f, bottom], send.at[1], recv.at[1], (s, fy)),
        remote(x.at[bottom], out.at[f, bottom], send.at[2], recv.at[2], (s, fx)),
        remote(x.at[top], out.at[f, top], send.at[3], recv.at[3], (s, fy)),
        remote(small, out_small.at[f], send.at[6], recv.at[6], (s, fx)),
        remote(small, out_small.at[f], send.at[7], recv.at[7], (s, fy)),
        remote(small, out_small.at[f], send.at[8], recv.at[8], (s, fd)),
    ]
    for copy in own:
        copy.start()
    local = pltpu.make_async_copy(x, out.at[f], local_sem)
    local.start()
    out_small[pl.ds(f, 1)] = small[...][None]
    own[0].wait_recv()
    on_y = remote(out.at[fx, top], out.at[fx, top], send.at[4], recv.at[4], (s, fy))
    on_y.start()
    own[1].wait_recv()
    on_x = remote(out.at[fy, bottom], out.at[fy, bottom], send.at[5], recv.at[5], (s, fx))
    on_x.start()
    own[0].wait_send()
    own[1].wait_send()
    for copy in own[2:]:
        copy.wait()
    on_y.wait()
    on_x.wait()
    local.wait()


def gather(x, small, collective_id):
    n = lax.axis_size("fsdp")
    if n != 4:
        return lax.all_gather(x, "fsdp"), lax.all_gather(small, "fsdp")
    rows, width = x.shape
    return pl.pallas_call(
        gather_kernel,
        out_shape=(
            jax.ShapeDtypeStruct((n, rows, width), x.dtype),
            jax.ShapeDtypeStruct((n,) + small.shape, F32),
        ),
        in_specs=[ANY, VMEM],
        out_specs=(ANY, VMEM),
        scratch_shapes=[
            pltpu.SemaphoreType.DMA,
            pltpu.SemaphoreType.DMA((9,)),
            pltpu.SemaphoreType.DMA((9,)),
        ],
        compiler_params=params(collective_id),
        name="gather_rows",
    )(x, small)


def reduce_kernel(p, small, out, out_small, from_x, from_y, pass_x, pass_y, small_in, send, recv):
    s, f, fx, fy, fd = plane()
    half = p.shape[1] // 2
    enter([(s, fx), (s, fy), (s, fd)])
    top, bottom = pl.ds(0, half), pl.ds(half, half)
    own = [
        remote(p.at[fd, top], from_x.at[0], send.at[0], recv.at[0], (s, fx)),
        remote(p.at[fd, bottom], from_y.at[0], send.at[1], recv.at[1], (s, fy)),
        remote(p.at[fx, top], from_x.at[1], send.at[2], recv.at[2], (s, fx)),
        remote(p.at[fy, bottom], from_y.at[1], send.at[3], recv.at[3], (s, fy)),
        remote(small, small_in.at[0], send.at[6], recv.at[6], (s, fx)),
        remote(small, small_in.at[1], send.at[7], recv.at[7], (s, fy)),
        remote(small, small_in.at[2], send.at[8], recv.at[8], (s, fd)),
    ]
    for copy in own:
        copy.start()
    own[0].wait_recv()
    pass_y[...] = (from_x[0].astype(F32) + p[pl.ds(fy, 1), :half][0].astype(F32)).astype(BF16)
    on_y = remote(pass_y, from_y.at[2], send.at[4], recv.at[4], (s, fy))
    on_y.start()
    own[1].wait_recv()
    pass_x[...] = (from_y[0].astype(F32) + p[pl.ds(fx, 1), half:][0].astype(F32)).astype(BF16)
    on_x = remote(pass_x, from_x.at[2], send.at[5], recv.at[5], (s, fx))
    on_x.start()
    own[2].wait_recv()
    own[3].wait_recv()
    out[:half] = p[pl.ds(f, 1), :half][0].astype(F32) + from_x[1].astype(F32)
    out[half:] = p[pl.ds(f, 1), half:][0].astype(F32) + from_y[1].astype(F32)
    for copy in own[4:]:
        copy.wait_recv()
    out_small[...] = (small[...] + small_in[0]) + (small_in[1] + small_in[2])
    on_y.wait_recv()
    out[:half] += from_y[2].astype(F32)
    on_x.wait_recv()
    out[half:] += from_x[2].astype(F32)
    for copy in own:
        copy.wait_send()
    on_y.wait_send()
    on_x.wait_send()


def reduce_rows(p, small, collective_id):
    n = lax.axis_size("fsdp")
    if n != 4:
        total = lax.psum_scatter(p, "fsdp", scatter_dimension=0, tiled=True)[0]
        return total.astype(F32), lax.psum(small, "fsdp")
    _, rows, width = p.shape
    half = (rows // 2, width)
    return pl.pallas_call(
        reduce_kernel,
        out_shape=(
            jax.ShapeDtypeStruct((rows, width), F32),
            jax.ShapeDtypeStruct(small.shape, F32),
        ),
        in_specs=[VMEM, VMEM],
        out_specs=(VMEM, VMEM),
        scratch_shapes=[
            pltpu.VMEM((3,) + half, BF16),
            pltpu.VMEM((3,) + half, BF16),
            pltpu.VMEM(half, BF16),
            pltpu.VMEM(half, BF16),
            pltpu.VMEM((3,) + small.shape, F32),
            pltpu.SemaphoreType.DMA((9,)),
            pltpu.SemaphoreType.DMA((9,)),
        ],
        compiler_params=params(collective_id),
        name="reduce_rows",
    )(p, small)


def start_exchange(total, gathered, send, recv, n_seq):
    s = lax.axis_index("seq")
    f = lax.axis_index("fsdp")
    copies = []
    for k in range(1, n_seq):
        peer = lax.rem(s + k, n_seq)
        copy = remote(total, gathered.at[s], send.at[k], recv.at[k], (peer, f))
        copy.start()
        copies.append(copy)
    gathered[pl.ds(s, 1)] = total[...][None]
    return copies


def seq_peers(n_seq):
    s = lax.axis_index("seq")
    f = lax.axis_index("fsdp")
    return [(lax.rem(s + k, n_seq), f) for k in range(1, n_seq)]


def lane_blocks(groups, chans):
    return [(g, slice(c, c + 128)) for g in range(groups) for c in range(0, chans, 128)]


def forward_scan_kernel(
    n_seq, in_raw, forget_raw, bounds, keep, state_b, before, a_ref, b_ref, total, gathered, send, recv
):
    groups, rows, chans = in_raw.shape
    part = rows // 8
    blocks = lane_blocks(groups, chans)
    s = lax.axis_index("seq")
    barrier = pltpu.get_barrier_semaphore()
    for peer in seq_peers(n_seq):
        pl.semaphore_signal(barrier, inc=1, device_id=peer, device_id_type=MESH)
    for n, (g, lanes) in enumerate(blocks):
        bound = bounds[:, lanes]
        forget = bound + (1.0 - bound) * jax.nn.sigmoid(forget_raw[g, :, lanes].astype(F32))
        value = in_raw[g, :, lanes].astype(F32)
        a_ref[n] = forget * keep[g]
        b_ref[n] = value * jax.nn.sigmoid(value) * (1.0 - forget)

    def step(i, carry):
        new = []
        at = pl.ds(i, 8, stride=part)
        for n, (product, state) in enumerate(carry):
            a = a_ref[n, at, :]
            state = a * state + b_ref[n, at, :]
            product = product * a
            a_ref[n, at, :] = product
            b_ref[n, at, :] = state
            new.append((product, state))
        return tuple(new)

    start = tuple((jnp.ones((8, 128), F32), jnp.zeros((8, 128), F32)) for _ in blocks)
    ends = lax.fori_loop(0, part, step, start)
    for n, (product, state) in enumerate(ends):
        p_all, s_all = product[0:1], state[0:1]
        for j in range(1, 8):
            p_all, s_all = p_all * product[j : j + 1], state[j : j + 1] + product[j : j + 1] * s_all
        total[2 * n : 2 * n + 1] = p_all
        total[2 * n + 1 : 2 * n + 2] = s_all
    pl.semaphore_wait(barrier, n_seq - 1)
    copies = start_exchange(total, gathered, send, recv, n_seq)
    for copy in copies:
        copy.wait()
    for n, (g, lanes) in enumerate(blocks):
        carry = jnp.zeros((1, 128), F32)
        for j in range(n_seq - 1):
            p_j = gathered[j, 2 * n : 2 * n + 1]
            s_j = gathered[j, 2 * n + 1 : 2 * n + 2]
            carry = jnp.where(j < s, s_j + p_j * carry, carry)
        before[g, 0:1, lanes] = carry
        product, state = ends[n]
        carries = [carry]
        for j in range(7):
            carries.append(state[j : j + 1] + product[j : j + 1] * carries[-1])
        for j in range(8):
            at = slice(j * part, (j + 1) * part)
            b_ref[n, at] = b_ref[n, at] + a_ref[n, at] * carries[j]
        state_b[g, :, lanes] = b_ref[n].astype(BF16)
        before[g, 1:rows, lanes] = b_ref[n, 0 : rows - 1]


def forward_scan(in_raw, forget_raw, bounds, keep, collective_id):
    n_seq = lax.axis_size("seq")
    groups, rows, chans = in_raw.shape
    blocks = groups * chans // 128
    return pl.pallas_call(
        functools.partial(forward_scan_kernel, n_seq),
        out_shape=(
            jax.ShapeDtypeStruct(in_raw.shape, BF16),
            jax.ShapeDtypeStruct(in_raw.shape, F32),
        ),
        in_specs=[VMEM] * 4,
        out_specs=(VMEM, VMEM),
        scratch_shapes=[
            pltpu.VMEM((blocks, rows, 128), F32),
            pltpu.VMEM((blocks, rows, 128), F32),
            pltpu.VMEM((2 * blocks, 128), F32),
            pltpu.VMEM((n_seq, 2 * blocks, 128), F32),
            pltpu.SemaphoreType.DMA((n_seq,)),
            pltpu.SemaphoreType.DMA((n_seq,)),
        ],
        compiler_params=params(collective_id),
        name="forward_scan",
    )(in_raw, forget_raw, bounds, keep)


def backward_scan_kernel(
    n_seq,
    d_state,
    in_raw,
    forget_raw,
    before,
    bounds,
    keep,
    d_in,
    d_forget_raw,
    d_bounds,
    p_ref,
    q_ref,
    total,
    gathered,
    send,
    recv,
):
    groups, rows, chans = in_raw.shape
    part = rows // 8
    blocks = lane_blocks(groups, chans)
    s = lax.axis_index("seq")
    barrier = pltpu.get_barrier_semaphore()
    for peer in seq_peers(n_seq):
        pl.semaphore_signal(barrier, inc=1, device_id=peer, device_id_type=MESH)
    for n, (g, lanes) in enumerate(blocks):
        bound = bounds[:, lanes]
        forget = bound + (1.0 - bound) * jax.nn.sigmoid(forget_raw[g, :, lanes].astype(F32))
        p_ref[n] = forget * keep[g]
        q_ref[n] = d_state[g, :, lanes].astype(F32)

    def step(i, carry):
        new = []
        at = pl.ds(part - 1 - i, 8, stride=part)
        for n, (product, message) in enumerate(carry):
            a = p_ref[n, at, :]
            acc = q_ref[n, at, :] + message
            p_ref[n, at, :] = product
            q_ref[n, at, :] = acc
            new.append((product * a, a * acc))
        return tuple(new)

    start = tuple((jnp.ones((8, 128), F32), jnp.zeros((8, 128), F32)) for _ in blocks)
    ends = lax.fori_loop(0, part, step, start)
    for n, (product, message) in enumerate(ends):
        p_all, m_all = product[7:8], message[7:8]
        for j in range(6, -1, -1):
            p_all, m_all = p_all * product[j : j + 1], message[j : j + 1] + product[j : j + 1] * m_all
        total[2 * n : 2 * n + 1] = p_all
        total[2 * n + 1 : 2 * n + 2] = m_all
    pl.semaphore_wait(barrier, n_seq - 1)
    copies = start_exchange(total, gathered, send, recv, n_seq)
    for copy in copies:
        copy.wait()
    d_bounds[...] = jnp.zeros((1, chans), F32)
    for n, (g, lanes) in enumerate(blocks):
        carry = jnp.zeros((1, 128), F32)
        for j in range(n_seq - 1, 0, -1):
            p_j = gathered[j, 2 * n : 2 * n + 1]
            m_j = gathered[j, 2 * n + 1 : 2 * n + 2]
            carry = jnp.where(j > s, m_j + p_j * carry, carry)
        product, message = ends[n]
        carries = [carry]
        for j in range(7, 0, -1):
            carries.append(message[j : j + 1] + product[j : j + 1] * carries[-1])
        carries = carries[::-1]
        for j in range(8):
            at = slice(j * part, (j + 1) * part)
            q_ref[n, at] = q_ref[n, at] + p_ref[n, at] * carries[j]
        acc = q_ref[n]
        bound = bounds[:, lanes]
        sigma_f = jax.nn.sigmoid(forget_raw[g, :, lanes].astype(F32))
        forget = bound + (1.0 - bound) * sigma_f
        value = in_raw[g, :, lanes].astype(F32)
        sigma_i = jax.nn.sigmoid(value)
        d_forget = acc * (before[g, :, lanes] * keep[g] - value * sigma_i)
        d_in[g, :, lanes] = (acc * (1.0 - forget) * silu_slope(value, sigma_i)).astype(BF16)
        d_sigma = d_forget * (1.0 - sigma_f)
        d_forget_raw[g, :, lanes] = (d_sigma * (1.0 - bound) * sigma_f).astype(BF16)
        d_bounds[:, lanes] += jnp.sum(d_sigma, 0, keepdims=True)


def backward_scan(d_state, in_raw, forget_raw, before, bounds, keep, collective_id):
    n_seq = lax.axis_size("seq")
    groups, rows, chans = in_raw.shape
    blocks = groups * chans // 128
    return pl.pallas_call(
        functools.partial(backward_scan_kernel, n_seq),
        out_shape=(
            jax.ShapeDtypeStruct(in_raw.shape, BF16),
            jax.ShapeDtypeStruct(in_raw.shape, BF16),
            jax.ShapeDtypeStruct((1, chans), F32),
        ),
        in_specs=[VMEM] * 6,
        out_specs=(VMEM, VMEM, VMEM),
        scratch_shapes=[
            pltpu.VMEM((blocks, rows, 128), F32),
            pltpu.VMEM((blocks, rows, 128), F32),
            pltpu.VMEM((2 * blocks, 128), F32),
            pltpu.VMEM((n_seq, 2 * blocks, 128), F32),
            pltpu.SemaphoreType.DMA((n_seq,)),
            pltpu.SemaphoreType.DMA((n_seq,)),
        ],
        compiler_params=params(collective_id),
        name="backward_scan",
    )(d_state, in_raw, forget_raw, before, bounds, keep)


def sum_all_kernel(n_seq, n_fsdp, x, out, middle, over_seq, over_fsdp, send, recv):
    s = lax.axis_index("seq")
    f = lax.axis_index("fsdp")
    along = [(lax.rem(s + k, n_seq), f) for k in range(1, n_seq)]
    across = [(s, lax.rem(f + k, n_fsdp)) for k in range(1, n_fsdp)]
    enter(along + across)
    copies = []
    for k, peer in enumerate(along):
        copy = remote(x, over_seq.at[k], send.at[k], recv.at[k], peer)
        copy.start()
        copies.append(copy)
    total = x[...]
    for k, copy in enumerate(copies):
        copy.wait_recv()
        total = total + over_seq[k]
    middle[...] = total
    later = []
    for k, peer in enumerate(across):
        slot = n_seq - 1 + k
        copy = remote(middle, over_fsdp.at[k], send.at[slot], recv.at[slot], peer)
        copy.start()
        later.append(copy)
    for k, copy in enumerate(later):
        copy.wait_recv()
        total = total + over_fsdp[k]
    out[...] = total
    for copy in copies + later:
        copy.wait_send()


def sum_all(x, collective_id):
    n_seq, n_fsdp = lax.axis_size("seq"), lax.axis_size("fsdp")
    count = n_seq + n_fsdp - 2
    return pl.pallas_call(
        functools.partial(sum_all_kernel, n_seq, n_fsdp),
        out_shape=jax.ShapeDtypeStruct(x.shape, F32),
        in_specs=[VMEM],
        out_specs=VMEM,
        scratch_shapes=[
            pltpu.VMEM(x.shape, F32),
            pltpu.VMEM((n_seq - 1,) + x.shape, F32),
            pltpu.VMEM((n_fsdp - 1,) + x.shape, F32),
            pltpu.SemaphoreType.DMA((count,)),
            pltpu.SemaphoreType.DMA((count,)),
        ],
        compiler_params=params(collective_id),
        name="sum_all",
    )(x)


def sum_over_seq(part):
    return lax.psum_scatter(part.astype(BF16), "seq", scatter_dimension=0, tiled=True).astype(F32)


def per_device(
    hidden,
    lengths,
    w_input,
    w_forget,
    w_gate_out,
    w_output,
    norm_gain,
    gate_gain,
    glu_gain,
    lower_table,
    w_glu_gate,
    w_glu_up,
    w_glu_down,
    cotangent,
):
    seq_index = lax.axis_index("seq")
    fsdp_index = lax.axis_index("fsdp")
    groups = lax.axis_size("fsdp")
    _, rows, width = hidden.shape
    chans = w_input.shape[1]
    units = w_glu_gate.shape[1]
    tokens = groups * rows
    small_shape = (round_up(groups, 8), round_up(rows, 128))

    def to_small(value):
        return jnp.pad(
            value, ((0, small_shape[0] - value.shape[0]), (0, small_shape[1] - value.shape[1]))
        )

    def dot(left, right):
        return jnp.dot(left, right, preferred_element_type=F32)

    def dot_t(left, right):
        return lax.dot_general(left, right, (((1,), (1,)), ((), ())), preferred_element_type=F32)

    def over_tokens(left, right):
        return lax.dot_general(left, right, (((0,), (0,)), ((), ())), preferred_element_type=F32)

    cotangent_all = lax.all_gather(cotangent[0], "fsdp").reshape(tokens, width)

    hidden_f = hidden[0].astype(F32)
    scale_one = lax.rsqrt(jnp.mean(hidden_f * hidden_f, -1, keepdims=True) + epsilon)
    normed = (hidden_f * scale_one * norm_gain).astype(BF16)
    normed_all, _ = gather(normed, jnp.zeros((8, 128), F32), 0)
    normed_all = normed_all.reshape(tokens, width)
    in_raw = dot(normed_all, w_input).astype(BF16).reshape(groups, rows, chans)
    forget_raw = dot(normed_all, w_forget).astype(BF16).reshape(groups, rows, chans)
    gate_raw = dot(normed_all, w_gate_out)

    bounds_full = lower_bound(lower_table)
    bounds = lax.dynamic_slice_in_dim(bounds_full, fsdp_index * chans, chans)[None]
    seq_starts = jnp.cumsum(lengths, axis=1) - lengths
    places = seq_index * rows + jnp.arange(rows, dtype=jnp.int32)
    starts = jnp.any(places[None, :, None] == seq_starts[:, None, :], axis=-1)
    keep = jnp.where(starts, 0.0, 1.0).astype(F32)[:, :, None]
    state_b, before = forward_scan(in_raw, forget_raw, bounds, keep, 1)

    state_f = state_b.astype(F32).reshape(tokens, chans)
    gain_slice = lax.dynamic_slice_in_dim(gate_gain, fsdp_index * chans, chans)
    sigma_g = jax.nn.sigmoid(gate_raw)
    silu_gate = gate_raw * sigma_g
    out_raw = (state_f * gain_slice * silu_gate).astype(BF16)
    squares = jnp.sum(state_f * state_f, -1).reshape(groups, rows)
    mixed_part = dot(out_raw, w_output).astype(BF16).reshape(groups, rows, width)
    mixed_raw, square_sum = reduce_rows(mixed_part, to_small(squares), 2)
    state_scale = lax.rsqrt(square_sum[:groups, :rows] / width + epsilon)
    own_scale = lax.dynamic_slice_in_dim(state_scale, fsdp_index, 1, 0)[0][:, None]
    scale_g = state_scale.reshape(tokens, 1)
    middle = hidden_f + own_scale * mixed_raw
    scale_two = lax.rsqrt(jnp.mean(middle * middle, -1, keepdims=True) + epsilon)
    normed_two = (middle * scale_two * glu_gain).astype(BF16)
    normed_two_all, _ = gather(normed_two, jnp.zeros((8, 128), F32), 3)
    normed_two_all = normed_two_all.reshape(tokens, width)

    gate_val = dot(normed_two_all, w_glu_gate)
    up_val = dot(normed_two_all, w_glu_up)
    sigma_u = jax.nn.sigmoid(gate_val)
    silu_u = gate_val * sigma_u
    activity = (silu_u * up_val).astype(BF16)
    down_grad = sum_over_seq(over_tokens(cotangent_all, activity))
    d_act = dot_t(cotangent_all, w_glu_down)
    d_gate = (d_act * up_val * silu_slope(gate_val, sigma_u)).astype(BF16)
    d_up = (d_act * silu_u).astype(BF16)
    pair_grad = sum_over_seq(
        jnp.concatenate(
            [
                over_tokens(normed_two_all, d_gate).astype(BF16),
                over_tokens(normed_two_all, d_up).astype(BF16),
            ],
            1,
        )
    )
    d_two_part = (dot_t(d_gate, w_glu_gate) + dot_t(d_up, w_glu_up)).astype(BF16)
    no_small = jnp.zeros((8, 128), F32)
    d_normed_two, _ = reduce_rows(d_two_part.reshape(groups, rows, width), no_small, 4)
    glu_part = dot(activity, w_glu_down).astype(BF16).reshape(groups, rows, width)
    glu_result = lax.psum_scatter(glu_part, "fsdp", scatter_dimension=0, tiled=True)[0]
    output = (middle + glu_result.astype(F32)).astype(BF16)[None]

    cotangent_f = cotangent[0].astype(F32)
    scaled_two = glu_gain * d_normed_two
    d_middle = (
        cotangent_f
        + scale_two * scaled_two
        - middle * scale_two**3 * jnp.mean(scaled_two * middle, -1, keepdims=True)
    )
    d_glu_gain = jnp.sum(d_normed_two * middle * scale_two, 0)
    d_mixed = d_middle.astype(BF16)
    own_dot = jnp.sum(d_mixed.astype(F32) * mixed_raw, -1)[None]
    d_mixed_all, dots = gather(d_mixed, to_small(own_dot), 5)
    d_mixed_all = d_mixed_all.reshape(tokens, width)
    dot_rows = dots[:, 0, :rows].reshape(tokens, 1)

    d_out = dot_t(d_mixed_all, w_output)
    scaled_state = state_f * scale_g
    d_gain_slice = jnp.sum(d_out * scaled_state * silu_gate, 0)
    d_scaled = d_out * gain_slice * silu_gate
    d_gate_raw = (d_out * scaled_state * gain_slice * silu_slope(gate_raw, sigma_g)).astype(BF16)
    d_state = scale_g * d_scaled - state_f * (scale_g**3 * (dot_rows / width))
    d_state = d_state.astype(BF16).reshape(groups, rows, chans)
    d_in, d_forget_raw, d_bounds = backward_scan(
        d_state, in_raw, forget_raw, before, bounds, keep, 6
    )
    d_in = d_in.reshape(tokens, chans)
    d_forget_raw = d_forget_raw.reshape(tokens, chans)

    d_normed_part = dot_t(d_in, w_input) + dot_t(d_forget_raw, w_forget)
    d_normed_part = (d_normed_part + dot_t(d_gate_raw, w_gate_out)).astype(BF16)
    out_gate = (out_raw.astype(F32) * scale_g).astype(BF16)
    mixer_grad = sum_over_seq(
        jnp.concatenate(
            [
                over_tokens(d_mixed_all, out_gate).astype(BF16),
                over_tokens(normed_all, d_in).astype(BF16),
                over_tokens(normed_all, d_forget_raw).astype(BF16),
                over_tokens(normed_all, d_gate_raw).astype(BF16),
            ],
            1,
        )
    )
    d_normed, _ = reduce_rows(d_normed_part.reshape(groups, rows, width), no_small, 7)
    scaled_one = norm_gain * d_normed
    d_hidden = (
        d_middle
        + scale_one * scaled_one
        - hidden_f * scale_one**3 * jnp.mean(scaled_one * hidden_f, -1, keepdims=True)
    )
    d_norm_gain = jnp.sum(d_normed * hidden_f * scale_one, 0)
    d_gain_full = lax.dynamic_update_slice(
        jnp.zeros((width,), F32), d_gain_slice, (fsdp_index * chans,)
    )
    d_bounds_full = lax.dynamic_update_slice(
        jnp.zeros((width,), F32), d_bounds[0], (fsdp_index * chans,)
    )
    sums = jnp.stack([d_norm_gain, d_glu_gain, d_gain_full, d_bounds_full])
    totals = sum_all(sums.reshape(8, width // 2), 8).reshape(4, width)
    _, bounds_pull = jax.vjp(lower_bound, lower_table)
    d_table = bounds_pull(totals[3])[0]
    return (
        output,
        d_hidden.astype(BF16)[None],
        mixer_grad[:, chans : 2 * chans],
        mixer_grad[:, 2 * chans : 3 * chans],
        mixer_grad[:, 3 * chans :],
        mixer_grad[:, :chans].T,
        totals[0],
        totals[2],
        totals[1],
        d_table,
        pair_grad[:, :units],
        pair_grad[:, units:],
        down_grad.T,
    )


def solution(mesh):
    rows_spec = P("fsdp", "seq", None)
    columns = P(None, "fsdp")
    placed = (
        rows_spec,
        P(),
        columns,
        columns,
        columns,
        P("fsdp", None),
        P(),
        P(),
        P(),
        P(),
        columns,
        columns,
        P("fsdp", None),
        rows_spec,
    )
    by_rows, by_columns = P("seq", "fsdp"), P("fsdp", "seq")
    return jax.shard_map(
        per_device,
        mesh=mesh,
        in_specs=placed,
        out_specs=(
            rows_spec,
            rows_spec,
            by_rows,
            by_rows,
            by_rows,
            by_columns,
            P(),
            P(),
            P(),
            P(),
            by_rows,
            by_rows,
            by_columns,
        ),
        check_vma=False,
    )
```

time: 1010 us -> 537 us (0.53)
  waiting for transfers between devices: 448 us -> 113 us
  Pallas kernels: 0 us -> 219 us
  local copies, waits for them, and re-layouts: 208 us -> 20.7 us
  blocking collectives: 107 us -> 0 us
  other arithmetic: 89.3 us -> 47.8 us
  starting transfers between devices: 18 us -> 0.67 us
    pallas_call x0 -> x9, Pallas kernels: none -> 219 us  [the longest x3 90.1 us: gather(): pl.pallas_call(gather_kernel, out_shape=(jax.ShapeDtypeStruct((n, rows, w...]
    unnamed x19 -> x6, waiting for transfers between devices: 200 us -> 0.77 us
    slice x136 -> x2, local copies, waits for them, and re-layouts: 151 us -> 3.88 us  [the longest x1 2.65 us: per_device(): pair_grad[:, units:]]
    all_gather x4 -> x1, waiting for transfers between devices: 106 us -> 0.01 us  [per_device(): cotangent_all = lax.all_gather(cotangent[0], 'fsdp').reshape(tokens, width)]
    all_to_all x3 -> x0, waiting for transfers between devices: 58.7 us -> none  [the longest x2 30.7 us: regroup_states(): lax.all_to_all(states, 'seq', split_axis=0, concat_axis=0, tiled=True)]
    psum x3 -> x0, blocking collectives: 58.3 us -> none  [the longest x1 40 us: per_device(): lax.psum((d_norm_gain, d_glu_gain, d_gain_full, d_bounds_full), ('seq', '...]
    all_to_all x1 -> x0, blocking collectives: 48.9 us -> none  [regroup_pairs(): return lax.all_to_all(pairs, 'seq', split_axis=0, concat_axis=0, tiled=True)]
    convert_element_type x15 -> x3, other arithmetic: 34 us -> 2.22 us  [the longest x1 1.05 us: per_device(): normed = (hidden_f * scale_one * norm_gain).astype(BF16)]
  transfers between devices with their start and end apart: 18 -> 5, of which waited for: 13 -> 1; matrix products, arithmetic and copies ran while one was open for 28% -> 28% of each run, Pallas kernels for 0% -> 42%
where the time goes in v1:
time: 537 us; the launch traced here: 528 us
  Pallas kernels  219 us (41%)
  waiting for transfers between devices  113 us (21%)
  matrix products  112 us (21%)
  other arithmetic  47.8 us (9%)
  local copies, waits for them, and re-layouts  20.7 us (4%)
  between operations  14.6 us (3%)
    reduce_scatter x3, waiting for transfers between devices, sum_over_seq(): lax.psum_scatter(part.astype(BF16), 'seq', scatter_dimension=0, tiled=True)  112 us
    pallas_call x3, Pallas kernels, gather(): pl.pallas_call(gather_kernel, out_shape=(jax.ShapeDtypeStruct((n, rows, w...  90.1 us
    pallas_call x3, Pallas kernels, reduce_rows(): pl.pallas_call(reduce_kernel, out_shape=(jax.ShapeDtypeStruct((rows, widt...  88.1 us
    dot_general x7, matrix products, dot(): return jnp.dot(left, right, preferred_element_type=F32)  41.4 us
    dot_general x7, matrix products, dot_t(): lax.dot_general(left, right, (((1,), (1,)), ((), ())), preferred_element_...  40.3 us
    dot_general x7, matrix products, over_tokens(): lax.dot_general(left, right, (((0,), (0,)), ((), ())), preferred_element_...  30.2 us
    pallas_call x1, Pallas kernels, sum_all(): pl.pallas_call(functools.partial(sum_all_kernel, n_seq, n_fsdp), out_shap...  17.4 us
    concatenate x1, other arithmetic, per_device(): jnp.concatenate([over_tokens(normed_two_all, d_gate).astype(BF16), over_t...  13.7 us
  transfers between devices with their start and end apart: 5, of which 1 were waited for; matrix products, arithmetic and copies ran while one was open for 28% of the time, Pallas kernels for 42%

profile of v1, /device:TPU:8, one launch (start us, length us, event | category | flops | bytes accessed | tf_op | source)
XLA Modules:
  0.0 527.8 jit_solution(17654355941397806880)
XLA Ops:
  17.2 40.1 %gather_rows.3 = (bf16[4,160,2048]{2,1,0:T(8,128)(2,1)}, f32[4,8,128]{2,1,0:T(8,128)}) custom-call(bf16[160,2048]{1,0:T(8,128)(2,1)} %fusion.4.x, f32[8,128]{1,0:T(8,128)} %broadcast_11_small.2.small), custom_call_target="tpu_custom_call" | custom-call | tf_op jit(solution)/shard_map/gather_rows/pallas_call | solution.py:108
  57.4 4.9 convolution_convert_fusion.7
  62.3 2.4 convolution_convert_fusion.8
  66.0 10.2 %forward_scan.1 = (bf16[4,160,512]{2,1,0:T(8,128)(2,1)}, f32[4,160,512]{2,1,0:T(8,128)}) custom-call(bf16[4,160,512]{2,1,0:T(8,128)(2,1)} %bitcast.133, bf16[4,160,512]{2,1,0:T(8,128)(2,1)} %bitcast.131, f32[1,512]{1,0:T(1,128)} %dynamic-slice_subtract_fusion.bounds, f32[4,160,1]{2,1,0:T(8,128)} %copy.46.keep), custom_call_target="tpu_custom_call" | custom-call | tf_op jit(solution)/shard_map/forward_scan/pallas_call | solution.py:282
  76.1 5.5 %fusion.15 = (bf16[640,512]{1,0:T(8,128)(2,1)}, f32[640,512]{1,0:T(8,128)}) fusion(bf16[4,160,512]{2,1,0:T(8,128)(2,1)} %get-tuple-element.27, f32[512]{0:T(512)S(1)} %dynamic_slice.10, bf16[640,2048]{1,0:T(8,128)(2,1)} %bitcast.149, bf16[2048,512]{1,0:T(8,128)(2,1)} %param.18), kind=kOutput, calls=%fused_computation.47 | convolution fusion | flops 1344798720 | bytes 7342080 | tf_op jit(solution)/shard_map/dot_general | solution.py:496
  82.5 4.1 convolution_convert_fusion.4
  86.6 27.3 %reduce_rows.3 = (f32[160,2048]{1,0:T(8,128)}, f32[8,256]{1,0:T(8,128)}) custom-call(bf16[4,160,2048]{2,1,0:T(8,128)(2,1)} %bitcast.129, f32[8,256]{1,0:T(8,128)} %pad.14.small), custom_call_target="tpu_custom_call" | custom-call | tf_op jit(solution)/shard_map/reduce_rows/pallas_call | solution.py:174
  117.4 25.8 %gather_rows.4 = (bf16[4,160,2048]{2,1,0:T(8,128)(2,1)}, f32[4,8,128]{2,1,0:T(8,128)}) custom-call(bf16[160,2048]{1,0:T(8,128)(2,1)} %multiply_convert_fusion.5.x, f32[8,128]{1,0:T(8,128)} %broadcast_11_small.2.small), custom_call_target="tpu_custom_call" | custom-call | tf_op jit(solution)/shard_map/gather_rows/pallas_call | solution.py:108
  143.2 9.6 %fusion.31 = f32[640,1408]{1,0:T(8,128)} fusion(bf16[640,2048]{1,0:T(8,128)(2,1)} %bitcast.154, bf16[2048,1408]{1,0:T(8,128)(2,1)} %param.25), kind=kOutput, calls=%fused_computation.101 | convolution fusion | flops 3690987520 | bytes 11993088 | tf_op jit(solution)/shard_map/dot_general | solution.py:496
  152.8 6.0 %fusion.30 = f32[640,1408]{1,0:T(8,128)} fusion(bf16[640,2048]{1,0:T(8,128)(2,1)S(1)} %bitcast.156, bf16[2048,1408]{1,0:T(8,128)(2,1)S(1)} %bitcast.147), kind=kOutput, calls=%fused_computation.100 | convolution fusion | flops 3690987520 | bytes 11993088 | tf_op jit(solution)/shard_map/dot_general | solution.py:496
  158.8 12.9 %multiply_convert_fusion = (bf16[640,1408]{1,0:T(8,128)(2,1)}, bf16[640,1408]{1,0:T(8,128)(2,1)}, bf16[640,1408]{1,0:T(8,128)(2,1)S(1)}) fusion(f32[640,1408]{1,0:T(8,128)} %fusion.30, f32[640,1408]{1,0:T(8,128)} %fusion.31, bf16[640,2048]{1,0:T(8,128)(2,1)} %bitcast.152, bf16[1408,2048]{1,0:T(8,128)(2,1)} %param.26), kind=kOutput, calls=%fused_computation.10 | convolution fusion | flops 3704504320 | bytes 21004288 | tf_op jit(solution)/shard_map/dot_general | solution.py:499
  171.7 8.9 %convolution_convert_fusion.3 = bf16[640,2048]{1,0:T(8,128)(2,1)} fusion(bf16[640,1408]{1,0:T(8,128)(2,1)S(1)} %get-tuple-element.102, bf16[1408,2048]{1,0:T(8,128)(2,1)} %param.26), kind=kOutput, calls=%fused_computation.15 | convolution fusion | flops 3692298240 | bytes 10190848 | tf_op jit(solution)/shard_map/dot_general | solution.py:496
  180.7 9.5 %fusion = bf16[2048,1408]{0,1:T(8,128)(2,1)} fusion(bf16[640,1408]{1,0:T(8,128)(2,1)} %copy-done.32, bf16[640,2048]{1,0:T(8,128)(2,1)} %bitcast.153), kind=kOutput, calls=%fused_computation.5 | convolution fusion | flops 3693871104 | bytes 10190848 | tf_op jit(solution)/shard_map/dot_general | solution.py:502
  190.3 7.2 %fusion.32 = f32[640,2048]{1,0:T(8,128)S(1)} fusion(bf16[640,1408]{1,0:T(8,128)(2,1)} %get-tuple-element.101, bf16[2048,1408]{1,0:T(8,128)(2,1)} %param.24), kind=kOutput, calls=%fused_computation.102 | convolution fusion | flops 3690987520 | bytes 12812288 | tf_op jit(solution)/shard_map/dot_general | solution.py:499
  197.5 8.4 %add_convert_fusion.1 = bf16[640,2048]{1,0:T(8,128)(2,1)} fusion(f32[640,2048]{1,0:T(8,128)S(1)} %fusion.32, bf16[640,1408]{1,0:T(8,128)(2,1)S(1)} %copy-done.31, bf16[2048,1408]{1,0:T(8,128)(2,1)} %param.25), kind=kOutput, calls=%fused_computation.7 | convolution fusion | flops 3693608960 | bytes 15433728 | tf_op jit(solution)/shard_map/dot_general | solution.py:499
  206.0 32.5 %reduce_rows.4 = (f32[160,2048]{1,0:T(8,128)}, f32[8,128]{1,0:T(8,128)}) custom-call(bf16[4,160,2048]{2,1,0:T(8,128)(2,1)} %bitcast.130, f32[8,128]{1,0:T(8,128)} %broadcast_11_small.2.small), custom_call_target="tpu_custom_call" | custom-call | tf_op jit(solution)/shard_map/reduce_rows/pallas_call | solution.py:174
  240.2 4.2 multiply_reduce_fusion.2
  245.0 24.3 %gather_rows.5 = (bf16[4,160,2048]{2,1,0:T(8,128)(2,1)}, f32[4,8,256]{2,1,0:T(8,128)}) custom-call(bf16[160,2048]{1,0:T(8,128)(2,1)} %get-tuple-element.96.x, f32[8,256]{1,0:T(8,128)} %pad.15.small), custom_call_target="tpu_custom_call" | custom-call | tf_op jit(solution)/shard_map/gather_rows/pallas_call | solution.py:108
  270.1 5.5 %multiply_convert_fusion.4 = (bf16[640,512]{1,0:T(8,128)(2,1)S(1)}, bf16[640,512]{1,0:T(8,128)(2,1)}, f32[512]{0:T(512)S(1)}) fusion(f32[640,512]{1,0:T(8,128)} %get-tuple-element.123, bf16[4,160,512]{2,1,0:T(8,128)(2,1)} %get-tuple-element.27, f32[640]{0:T(1024)S(1)} %mul.304, f32[512]{0:T(512)S(1)} %dynamic_slice.10, f32[640]{0:T(1024)S(1)} %fusion.25, ...), kind=kOutput, calls=%fused_computation.54 | convolution fusion | flops 1349385728 | bytes 8004608 | tf_op jit(solution)/shard_map/dot_general | solution.py:499
  275.6 13.5 %backward_scan.1 = (bf16[4,160,512]{2,1,0:T(8,128)(2,1)}, bf16[4,160,512]{2,1,0:T(8,128)(2,1)}, f32[1,512]{1,0:T(1,128)}) custom-call(bf16[4,160,512]{2,1,0:T(8,128)(2,1)} %bitcast.137, bf16[4,160,512]{2,1,0:T(8,128)(2,1)} %bitcast.134, bf16[4,160,512]{2,1,0:T(8,128)(2,1)} %bitcast.132, f32[4,160,512]{2,1,0:T(8,128)} %get-tuple-element.34.before, ...), custom_call_target="tpu_custom_call" | custom-call | tf_op jit(solution)/shard_map/backward_scan/pallas_call | solution.py:389
  289.1 3.0 bitcast_convert_fusion.1
  297.8 4.0 pad_maximum_fusion.1
  302.4 7.1 %convolution_convert_fusion.1 = bf16[2048,1408]{0,1:T(8,128)(2,1)S(1)} fusion(bf16[640,2048]{1,0:T(8,128)(2,1)} %bitcast.155, bf16[640,1408]{1,0:T(8,128)(2,1)} %get-tuple-element.100), kind=kOutput, calls=%fused_computation.3 | convolution fusion | flops 3693871104 | bytes 10190848 | tf_op jit(solution)/shard_map/dot_general | solution.py:502
  309.6 5.0 convolution_convert_fusion.2
  314.5 13.7 %pad_maximum_fusion = bf16[2048,2816]{0,1:T(8,128)(2,1)} fusion(bf16[2048,1408]{0,1:T(8,128)(2,1)S(1)} %convolution_convert_fusion.1, bf16[2048,1408]{0,1:T(8,128)(2,1)S(1)} %convolution_convert_fusion.2), kind=kLoop, calls=%fused_computation | loop fusion | flops 23068672 | bytes 23068672 | tf_op jit(solution)/shard_map/concatenate | solution.py:550
  333.3 3.2 add_convert_fusion
  336.5 28.3 %reduce_rows.5 = (f32[160,2048]{1,0:T(8,128)}, f32[8,128]{1,0:T(8,128)}) custom-call(bf16[4,160,2048]{2,1,0:T(8,128)(2,1)} %bitcast.127, f32[8,128]{1,0:T(8,128)} %broadcast_11_small.2.small), custom_call_target="tpu_custom_call" | custom-call | tf_op jit(solution)/shard_map/reduce_rows/pallas_call | solution.py:174
  367.5 17.4 %sum_all.1 = f32[8,1024]{1,0:T(8,128)} custom-call(f32[8,1024]{1,0:T(8,128)} %reshape.215.x), custom_call_target="tpu_custom_call" | custom-call | tf_op jit(solution)/shard_map/sum_all/pallas_call | solution.py:444
  394.1 2.3 convert_bitcast_fusion
  401.7 112.2 %reduce-scatter.9.cloned.1.call-done = bf16[256,2816]{0,1:T(8,128)(2,1)} async-done(((bf16[2048,2816]{0,1:T(8,128)(2,1)}), bf16[256,2816]{0,1:T(8,128)(2,1)}) %reduce-scatter.9.cloned.1.call-update) | async-done | bytes 1441808 | tf_op jit(solution)/shard_map/reduce_scatter | solution.py:462
  513.8 2.6 fusion.27
  516.5 3.0 copy.52
  (148 shorter events, 48.7 us)
Async XLA Ops:
  7.2 75.3 %copy-start = (bf16[512,2048]{1,0:T(8,128)(2,1)S(1)}, bf16[512,2048]{1,0:T(8,128)(2,1)}, u32[]{:S(2)}) copy-start(bf16[512,2048]{1,0:T(8,128)(2,1)} %param.19) | copy-start | bytes 6291460
  7.2 8.4 %copy-start.2 = (bf16[1,160,2048]{2,1,0:T(8,128)(2,1)S(1)}, bf16[1,160,2048]{2,1,0:T(8,128)(2,1)}, u32[]{:S(2)}) copy-start(bf16[1,160,2048]{2,1,0:T(8,128)(2,1)} %param.14) | copy-start | bytes 1966084
  7.2 8.4 %copy-start.17 = (f32[2048]{0:T(1024)S(1)}, f32[2048]{0:T(1024)}, u32[]{:S(2)}) copy-start(f32[2048]{0:T(1024)} %param.20) | copy-start | bytes 24580
  7.2 151.6 %all-gather.2.cloned.1.call-start = ((), (), s32[]{:S(2)}) async-start(), calls=%async_computation.4 | async-start | bytes 3276800 | tf_op jit(solution)/shard_map/all_gather | solution.py:504
  8.0 232.2 %reduce-scatter.13.cloned.1.call-start = ((), (), s32[]{:S(2)}) async-start(), calls=%async_computation.8 | async-start | bytes 3276800
  9.9 52.3 %copy-start.20 = (f32[160]{0:T(256)}, f32[160]{0:T(256)S(1)}, u32[]{:S(2)}) copy-start(f32[160]{0:T(256)S(1)} %get-tuple-element.119) | copy-start | bytes 1924
  57.3 4.9 copy-start.10
  57.3 4.9 copy-start.24
  76.1 5.5 %copy-start.14 = (bf16[4,160,512]{2,1,0:T(8,128)(2,1)S(1)}, bf16[4,160,512]{2,1,0:T(8,128)(2,1)}, u32[]{:S(2)}) copy-start(bf16[4,160,512]{2,1,0:T(8,128)(2,1)} %get-tuple-element.27) | copy-start | bytes 1966084
  86.6 28.1 %copy-start.3 = (bf16[1,160,2048]{2,1,0:T(8,128)(2,1)S(1)}, bf16[1,160,2048]{2,1,0:T(8,128)(2,1)}, u32[]{:S(2)}) copy-start(bf16[1,160,2048]{2,1,0:T(8,128)(2,1)} %param.14) | copy-start | bytes 1966084
  116.4 36.5 %slice-start = ((s8[5767168]{0:T(1024)(128)(4,1)}), s8[1572864]{0:T(1024)(128)(4,1)S(1)}, s32[]{:S(2)}) async-start(s8[5767168]{0:T(1024)(128)(4,1)} %bitcast.146), calls=%async_computation.9 | async-start | bytes 3145728
  143.2 9.6 %slice-start.1 = ((s8[5767168]{0:T(1024)(128)(4,1)}), s8[4194304]{0:T(1024)(128)(4,1)S(1)}, s32[]{:S(2)}) async-start(s8[5767168]{0:T(1024)(128)(4,1)} %bitcast.146), calls=%async_computation.10 | async-start | bytes 8388608
  143.2 9.6 %copy-start.26 = (bf16[4,160,2048]{2,1,0:T(8,128)(2,1)S(1)}, bf16[4,160,2048]{2,1,0:T(8,128)(2,1)}, u32[]{:S(2)}) copy-start(bf16[4,160,2048]{2,1,0:T(8,128)(2,1)} %get-tuple-element.30) | copy-start | bytes 7864324
  171.7 8.9 %copy-start.32 = (bf16[640,1408]{1,0:T(8,128)(2,1)}, bf16[640,1408]{1,0:T(8,128)(2,1)S(1)}, u32[]{:S(2)}) copy-start(bf16[640,1408]{1,0:T(8,128)(2,1)S(1)} %get-tuple-element.102) | copy-start | bytes 5406724
  180.7 213.5 %reduce-scatter.11.cloned.1.call-start = ((), (), s32[]{:S(2)}) async-start(), calls=%async_computation.7 | async-start | bytes 6488064 | tf_op jit(solution)/shard_map/reduce_scatter | solution.py:462
  190.2 206.2 %reduce-scatter.7.cloned.1.call-start = ((), (), s32[]{:S(2)}) async-start(), calls=%async_computation.5 | async-start | bytes 9437184 | tf_op jit(solution)/shard_map/reduce_scatter | solution.py:462
  190.3 7.2 %copy-start.31 = (bf16[640,1408]{1,0:T(8,128)(2,1)S(1)}, bf16[640,1408]{1,0:T(8,128)(2,1)}, u32[]{:S(2)}) copy-start(bf16[640,1408]{1,0:T(8,128)(2,1)} %get-tuple-element.100) | copy-start | bytes 5406724
  275.6 13.5 %copy-start.25 = (bf16[4,160,2048]{2,1,0:T(8,128)(2,1)S(1)}, bf16[4,160,2048]{2,1,0:T(8,128)(2,1)}, u32[]{:S(2)}) copy-start(bf16[4,160,2048]{2,1,0:T(8,128)(2,1)} %get-tuple-element.26) | copy-start | bytes 7864324
  289.1 3.0 copy-start.13
  301.9 7.7 %copy-start.30 = (bf16[640,1408]{1,0:T(8,128)(2,1)S(1)}, bf16[640,1408]{1,0:T(8,128)(2,1)}, u32[]{:S(2)}) copy-start(bf16[640,1408]{1,0:T(8,128)(2,1)} %get-tuple-element.101) | copy-start | bytes 5406724
  301.9 211.9 %reduce-scatter.9.cloned.1.call-start = ((), (), s32[]{:S(2)}) async-start(), calls=%async_computation.6 | async-start | bytes 12976128 | tf_op jit(solution)/shard_map/reduce_scatter | solution.py:462
  302.4 7.1 %copy-start.27 = (bf16[4,160,2048]{2,1,0:T(8,128)(2,1)S(1)}, bf16[4,160,2048]{2,1,0:T(8,128)(2,1)}, u32[]{:S(2)}) copy-start(bf16[4,160,2048]{2,1,0:T(8,128)(2,1)} %get-tuple-element.30) | copy-start | bytes 7864324
  336.5 28.4 %copy-start.23 = (f32[1,512]{1,0:T(1,128)S(1)}, f32[1,512]{1,0:T(1,128)}, u32[]{:S(2)}) copy-start(f32[1,512]{1,0:T(1,128)} %get-tuple-element.38) | copy-start | bytes 6148
  336.5 28.5 %copy-start.4 = (bf16[1,160,2048]{2,1,0:T(8,128)(2,1)S(1)}, bf16[1,160,2048]{2,1,0:T(8,128)(2,1)}, u32[]{:S(2)}) copy-start(bf16[1,160,2048]{2,1,0:T(8,128)(2,1)} %param.14) | copy-start | bytes 1966084
  336.5 28.5 %copy-start.18 = (f32[2048]{0:T(1024)S(1)}, f32[2048]{0:T(1024)}, u32[]{:S(2)}) copy-start(f32[2048]{0:T(1024)} %param.20) | copy-start | bytes 24580
  336.5 28.5 %copy-start.21 = (f32[160]{0:T(256)S(1)}, f32[160]{0:T(256)}, u32[]{:S(2)}) copy-start(f32[160]{0:T(256)} %copy-done.20) | copy-start | bytes 1924
  364.8 24.5 %copy-start.16 = (f32[2048]{0:T(1024)S(1)}, f32[2048]{0:T(1024)}, u32[]{:S(2)}) copy-start(f32[2048]{0:T(1024)} %copy-done.15) | copy-start | bytes 24580
  364.8 28.0 %copy-start.6 = (f32[160,2048]{1,0:T(8,128)S(1)}, f32[160,2048]{1,0:T(8,128)}, u32[]{:S(2)}) copy-start(f32[160,2048]{1,0:T(8,128)} %get-tuple-element.37) | copy-start | bytes 3932164
  364.8 28.0 %copy-start.7 = (f32[160,2048]{1,0:T(8,128)S(1)}, f32[160,2048]{1,0:T(8,128)}, u32[]{:S(2)}) copy-start(f32[160,2048]{1,0:T(8,128)} %get-tuple-element.97) | copy-start | bytes 3932164
  364.9 28.0 %copy-start.22 = (f32[160]{0:T(256)S(1)}, f32[160]{0:T(256)}, u32[]{:S(2)}) copy-start(f32[160]{0:T(256)} %get-tuple-element.118) | copy-start | bytes 1924
  397.7 3.0 copy-start.5
  516.5 4.6 copy-start.1
  (8 other events, 13.8 us)
Sparse Core Ops, SparseCore 0:
  9.9 54.2 all-gather.1
  180.8 46.7 reduce-scatter.12
  229.9 64.1 reduce-scatter.10
  302.0 91.4 reduce-scatter.6
  395.6 118.1 reduce-scatter.8
